TPU v7x, 32 devices: a whole 2x2x4 slice. The times are simulated.
32 devices in a mesh: leaf: 16 (over z, y, x), grp: 2 (over core).
Axes of the slice: x: 2, y: 2, z: 4, core: 2. Of those that a mesh axis runs over, the one named last changes fastest.
Arguments:
- points: bfloat16 [256, 32768], P(None, ('leaf', 'grp')), may hold values from -6 to 6
- charges: bfloat16 [64, 32768], P(None, ('leaf', 'grp')), may hold values from -6 to 6
- order: int32 [32768], P(('leaf', 'grp')), may hold values from 0 to 1023, as said below
- near_mask: int32 [32, 5], P(('leaf', 'grp')), may hold values from 0 to 1, as said below
- skeletons: int32 [32, 5, 128], P(('leaf', 'grp')), may hold values from 0 to 1023, as said below
- leaf_interp: bfloat16 [128, 32768], P(None, ('leaf', 'grp')), may hold values from -0.5 to 0.5
- transfer: bfloat16 [32, 4, 128, 128], P(('leaf', 'grp')), as said below
Outputs:
- potentials: float32 [64, 32768], P(None, ('leaf', 'grp'))
Inputs may be any that keep to these rules, and one draw needn't show every extreme that they name: `order`: within each block of 1024 consecutive entries, a permutation of 0 to 1023. `near_mask`: entry 2 of every row is 1; an entry is 0 where it points outside the leaf coordinates; the pattern is symmetric: block b marks the block k leaf coordinates away exactly when that block marks b. Level 0 holds 128 different rows of the block; level j >= 1 holds 128 different positions of 0 to 255 in the two children's skeletons; the set of a node is the same on every block of that node. `transfer`: the matrix of a node is the same on every block of that node.
All inputs are finite; a program needn't handle non-finite values.
Results may differ from a plain program's by a relative error of at most 0.0019.
Values may be sent and summed in bfloat16 or wider, within the bound.
No kernel may reach another device: no remote copies, remote signals or barrier semaphores. Data moves between devices by JAX's collectives and lax.ppermute only.
A program may use at most 64 MiB of HBM per device.

v0:
```python
import functools

import jax
import jax.numpy as jnp
from jax import lax
from jax.experimental import pallas as pl
from jax.experimental.pallas import tpu as pltpu
from jax.sharding import PartitionSpec as P

REACH = 2
BF16 = jnp.bfloat16
F32 = jnp.float32
LOG2E = 1.4426950408889634
HIGHEST = lax.Precision.HIGHEST
PAD = 16
VMEM_LIMIT = 40 * 1024 * 1024
START_VMEM = 56 * 1024 * 1024

NN = ((1,), (0,))
NT = ((1,), (1,))
TN = ((0,), (0,))


def dot(left, right, contract=NN, precision=None):
    return lax.dot_general(
        left, right, (contract, ((), ())), preferred_element_type=F32, precision=precision
    )


def halves(value):
    high = value.astype(BF16)
    return high, (value - high.astype(F32)).astype(BF16)


def dot_split(left, right, contract=NN):
    rows = left.shape[0]
    both = dot(jnp.concatenate(halves(left), axis=0), right, contract)
    return both[:rows] + both[rows:]


def row_norms(points):
    wide = points.astype(F32)
    return jnp.sum(wide * wide, axis=0, keepdims=True)


def column_norms(points):
    wide = points.astype(F32)
    high, low = halves(wide * wide)
    ones = jnp.ones((points.shape[0], 128), BF16)
    return dot(high, ones, TN) + dot(low, ones, TN)


def one_hot(index, rows, first):
    place = lax.broadcasted_iota(jnp.int32, (rows, index.shape[1]), 0) + first
    return jnp.where(place == index, 1.0, 0.0).astype(BF16)


def small_kernel(source, target):
    scale = 2.0 * LOG2E / source.shape[0]
    inner = dot(source, target, TN)
    squares = column_norms(source)[:, : target.shape[1]] + row_norms(target)
    return jnp.exp2(scale * (2.0 * inner - squares))


def pick(first, second, index, bit):
    count = first.shape[1]
    table = jnp.concatenate(
        [one_hot(index, count, count * bit), one_hot(index, count, count * (1 - bit))], axis=0
    )
    return dot(jnp.concatenate([first, second], axis=1), table).astype(BF16)


def write_message(weights, coords, matrix, message_ref, passed_ref):
    dimension, sides = coords.shape[0], weights.shape[0]
    passed = dot_split(weights, matrix, NT)
    message_ref[:dimension] = coords
    message_ref[dimension : dimension + sides] = weights.astype(BF16)
    message_ref[dimension + sides : dimension + 2 * sides] = passed.astype(BF16)
    passed_ref[...] = passed


def start_kernel(*refs):
    inputs, outs, held = refs[:7], refs[7:12], refs[12:19]
    made, sems, out_sems = refs[19:24], refs[24], refs[25]
    copies = [
        pltpu.make_async_copy(source, target, sems.at[number])
        for number, (source, target) in enumerate(zip(inputs, held))
    ]
    for copy in copies:
        copy.start()
    stores = [
        pltpu.make_async_copy(source, target, out_sems.at[number])
        for number, (source, target) in enumerate(zip(made, outs))
    ]
    order, skeletons, mask, charges, points, interp, transfer = held
    ordered_ref, coords_ref, marks_ref, message_ref, passed_ref = made
    dimension, rows = points.shape
    sides, count = passed_ref.shape
    for copy in copies[:4]:
        copy.wait()
    width = rows // 4
    for column in range(0, rows, width):
        table = one_hot(order[:, column : column + width], rows, 0)
        ordered_ref[:, column : column + width] = dot(charges[...], table).astype(BF16)
    stores[0].start()
    copies[4].wait()
    coords = dot(points[...], one_hot(skeletons[0], rows, 0)).astype(BF16)
    coords_ref[...] = coords
    stores[1].start()
    lane = lax.broadcasted_iota(jnp.int32, (1, count), 1)
    pattern = jnp.zeros((1, count), jnp.int32)
    for offset in range(mask.shape[1]):
        pattern = jnp.where(lane == offset, mask[:, offset : offset + 1], pattern)
    marks = jnp.broadcast_to(pattern.astype(F32), (PAD, count)).astype(BF16)
    marks_ref[...] = marks
    message_ref[dimension + 2 * sides :] = marks
    stores[2].start()
    copies[5].wait()
    weights = dot(ordered_ref[...], interp[...], NT)
    copies[6].wait()
    write_message(weights, coords, transfer[0], message_ref, passed_ref)
    stores[3].start()
    stores[4].start()
    for store in stores:
        store.wait()


def marked(marks, offset):
    rows = marks.astype(F32)
    lane = lax.broadcasted_iota(jnp.int32, rows.shape, 1)
    return jnp.max(jnp.where(lane == REACH + offset, rows, 0.0)) > 0.5


def round_kernel(level, last, skeletons, transfer, coords, passed, message, *outs):
    dimension = coords.shape[0]
    sides = passed.shape[0]
    bit = (lax.axis_index("leaf") >> level) & 1
    joined = pick(coords[...], message[:dimension], skeletons[level + 1], bit)
    span = slice(dimension + sides, dimension + 2 * sides)
    weights = passed[...] + message[span].astype(F32)
    if last:
        outs[0][:dimension] = joined
        outs[0][dimension:] = weights.astype(BF16)
        return
    outs[0][...] = joined
    write_message(weights, joined, transfer[level + 1], outs[1], outs[2])


def sibling_term(coords, message, sides):
    dimension = coords.shape[0]
    weights = message[dimension : dimension + sides].astype(F32)
    return dot(weights, small_kernel(message[:dimension], coords[...]), NN, HIGHEST)


def early_terms_kernel(levels, sides, transfer, *refs):
    outs = refs[2 * (levels - 1) :]
    for level in range(levels - 1):
        outs[level][...] = sibling_term(refs[2 * level], refs[2 * level + 1], sides)
    product = transfer[levels - 1].astype(F32)
    for level in range(levels - 2, -1, -1):
        product = dot(product, transfer[level].astype(F32), NN, HIGHEST)
    outs[-1][...] = product


def last_term_kernel(sides, transfer, coords, message, *refs):
    terms, potential_ref = refs[:-1], refs[-1]
    potential = sibling_term(coords, message, sides)
    for level in range(len(terms) - 1, -1, -1):
        potential = dot_split(potential, transfer[level]) + terms[level][...]
    potential_ref[...] = potential


def turn_kernel(points, tall_ref, norms_ref):
    dimension, rows = points.shape
    tall_ref[...] = jnp.transpose(points[...])
    square = jnp.square(tall_ref[...].astype(F32))
    norms = jnp.sum(square, axis=1, keepdims=True) * (2.0 * LOG2E / dimension)
    norms_ref[...] = jnp.broadcast_to(norms, (rows, 128))


def bands(tall, norms, wide):
    rows, dimension = tall.shape
    scale = 2.0 * LOG2E / dimension
    height = min(256, rows)
    target_norms = row_norms(wide[...]) * scale
    for row in range(0, rows, height):
        band = slice(row, row + height)
        inner = dot(tall[band], wide[...])
        squares = jnp.tile(norms[band], (1, rows // 128)) + target_norms
        yield band, jnp.exp2((2.0 * scale) * inner - squares).astype(BF16)


def self_kernel(tall, norms, wide, ordered, near_ref):
    for band, tile in bands(tall, norms, wide):
        near_ref[:, band] = dot(ordered[...], tile, NT)


def back_kernel(tall, norms, ordered, back_wide, back_ordered, marks, near, near_ref, held_ref):
    near_ref[...] = near[...]
    used = marked(marks[...], -2)

    @pl.when(used)
    def _():
        for band, tile in bands(tall, norms, back_wide):
            near_ref[:, band] += dot(back_ordered[...], tile, NT)
            part = dot(ordered[:, band], tile)
            if band.start:
                held_ref[...] += part
            else:
                held_ref[...] = part

    @pl.when(jnp.logical_not(used))
    def _():
        held_ref[...] = jnp.zeros_like(held_ref)


def pair_kernel(wide, ordered, side_tall, side_norms, side_ordered, back_wide, back_ordered,
                marks, message, near, held, near_ref, back_ref, side_ref, sum_ref):
    odd = lax.rem(lax.axis_index("leaf"), 2)
    go_odd = jnp.logical_and(odd == 1, marked(message[message.shape[0] - PAD :], -1))
    go_even = jnp.logical_and(odd == 0, marked(marks[...], 1))

    def pair(other_wide, other_ordered, base, out_ref):
        for band, tile in bands(side_tall, side_norms, other_wide):
            side_ref[:, band] = dot(other_ordered[...], tile, NT).astype(BF16)
            part = dot(side_ordered[:, band], tile)
            if band.start == 0:
                part = part + base[...]
            if band.stop < wide.shape[1]:
                sum_ref[...] = part if band.start == 0 else sum_ref[...] + part
            else:
                if band.start:
                    part = part + sum_ref[...]
                out_ref[...] = part.astype(out_ref.dtype)

    @pl.when(go_odd)
    def _():
        pair(back_wide, back_ordered, held, back_ref)
        near_ref[...] = near[...]

    @pl.when(go_even)
    def _():
        pair(wide, ordered, near, near_ref)
        back_ref[...] = held[...].astype(BF16)

    @pl.when(jnp.logical_not(jnp.logical_or(go_odd, go_even)))
    def _():
        near_ref[...] = near[...]
        back_ref[...] = held[...].astype(BF16)
        side_ref[...] = jnp.zeros_like(side_ref)


def far_kernel(others, own_top, potential, product, interp, near, *refs):
    tops, out_ref = refs[:others], refs[-1]
    sides = out_ref.shape[0]
    dimension = own_top.shape[0] - sides
    total = potential[...]
    above = None
    for top in tops:
        part = dot(
            top[dimension:].astype(F32),
            small_kernel(top[:dimension], own_top[:dimension]),
            NN,
            HIGHEST,
        )
        above = part if above is None else above + part
    if above is not None:
        total = total + dot(above, product[...], NN, HIGHEST)
    out_ref[...] = near[...] + dot_split(total, interp[...])


def total_kernel(here, back, side, out_ref):
    out_ref[...] = here[...] + (back[...].astype(F32) + side[...].astype(F32))


def call(kernel, outs, args, scratch=(), anywhere=False, flops=0, exps=0, name=None):
    vmem = pl.BlockSpec(memory_space=pltpu.VMEM)
    rest = pl.BlockSpec(memory_space=pl.ANY) if anywhere else vmem
    moved = 0 if anywhere else sum(a.size * a.dtype.itemsize for a in list(args) + list(outs))
    return pl.pallas_call(
        kernel,
        out_shape=outs,
        in_specs=[rest] * len(args),
        out_specs=[rest if anywhere else vmem] * len(outs),
        scratch_shapes=list(scratch),
        compiler_params=pltpu.CompilerParams(
            vmem_limit_bytes=START_VMEM if anywhere else VMEM_LIMIT
        ),
        cost_estimate=pl.CostEstimate(flops=flops, bytes_accessed=moved, transcendentals=exps),
        name=name,
    )(*args)


def swapped(value, axis, flip):
    count = lax.axis_size(axis)
    return lax.ppermute(value, axis, [(place, place ^ flip) for place in range(count)])


def rotated(value, axis, turn):
    count = lax.axis_size(axis)
    return lax.ppermute(value, axis, [(place, (place + turn) % count) for place in range(count)])


def shape(dims, dtype):
    return jax.ShapeDtypeStruct(dims, dtype)


def local(points, charges, order, near_mask, skeletons, leaf_interp, transfer):
    dimension, rows = points.shape
    sides, count = charges.shape[0], leaf_interp.shape[0]
    leaves, groups = lax.axis_size("leaf"), lax.axis_size("grp")
    levels = leaves.bit_length() - 1
    skeletons = jnp.transpose(skeletons, (1, 0, 2))
    transfer = transfer[0]
    block_sums = shape((sides, rows), F32)
    block_values = shape((sides, rows), BF16)
    node_points = shape((dimension, count), BF16)
    node_sums = shape((sides, count), F32)
    tile_flops = 2 * rows * rows * (dimension + 2 * sides)

    back_points = rotated(points, "leaf", 2)

    inputs = [order.reshape(1, rows), skeletons, near_mask, charges, points, leaf_interp, transfer]
    made = [
        block_values,
        node_points,
        shape((PAD, count), BF16),
        shape((dimension + 2 * sides + PAD, count), BF16),
        node_sums,
    ]
    ordered, coords, marks, message, passed = call(
        start_kernel,
        made,
        inputs,
        scratch=[pltpu.VMEM(value.shape, value.dtype) for value in inputs + made]
        + [pltpu.SemaphoreType.DMA((len(inputs),)), pltpu.SemaphoreType.DMA((len(made),))],
        anywhere=True,
        name="start",
    )
    def turned(value):
        return call(
            turn_kernel,
            [shape((rows, dimension), BF16), shape((rows, 128), F32)],
            [value],
            flops=dimension * rows,
            name="turn",
        )

    tall, norms = turned(lax.optimization_barrier((points, passed))[0])
    (near,) = call(
        self_kernel,
        [block_sums],
        [tall, norms, points, ordered],
        flops=tile_flops,
        exps=rows * rows,
        name="self_tile",
    )

    history = []
    for level in range(levels):
        received = swapped(message, "leaf", 1 << level)
        if level == 0:
            received, near, early_points = lax.optimization_barrier((received, near, points))
            first_received = received
            side_points = swapped(early_points, "leaf", 1)
        if level == 1:
            received, back_points = lax.optimization_barrier((received, back_points))
        history += [coords, received]
        if level == levels - 1:
            near, held = call(
                back_kernel,
                [block_sums, block_sums],
                [tall, norms, ordered, back_points, back_ordered, marks]
                + [lax.optimization_barrier((near, passed))[0]],
                flops=tile_flops,
                exps=rows * rows,
                name="back_tile",
            )
            passed, held = lax.optimization_barrier((passed, held))
        last = level == levels - 1
        if last:
            side_tall, side_norms = turned(side_points)
            near, back, side = call(
                pair_kernel,
                [block_sums, block_values, block_values],
                [points, ordered, side_tall, side_norms, side_ordered, back_points, back_ordered]
                + [marks, first_received, lax.optimization_barrier((near, passed))[0], held],
                scratch=[pltpu.VMEM((sides, rows), F32)],
                flops=tile_flops,
                exps=rows * rows,
                name="pair_tile",
            )
            passed, near = lax.optimization_barrier((passed, near))
            back = rotated(back, "leaf", -2)
            side = swapped(side, "leaf", 1)
            *terms, product = call(
                functools.partial(early_terms_kernel, levels, sides),
                [node_sums] * (levels - 1) + [shape((count, count), F32)],
                [transfer] + history[:-2],
                flops=8 * levels * dimension * count * count,
                exps=levels * count * count,
                name="early_terms",
            )
            passed, terms, product = lax.optimization_barrier((passed, terms, product))
        if last:
            outs = [shape((dimension + sides, count), BF16)]
        else:
            outs = [node_points, shape((dimension + 2 * sides, count), BF16), node_sums]
        results = call(
            functools.partial(round_kernel, level, last),
            outs,
            [skeletons, transfer, coords, passed, received],
            flops=8 * dimension * count * count,
            name="join_level",
        )
        if not last:
            coords, message, passed = results
        if level == min(1, levels - 1):
            sent = lax.optimization_barrier((ordered, results[-1]))[0]
            back_ordered = rotated(sent, "leaf", 2)
            side_ordered = swapped(sent, "leaf", 1)
    own_top = results[0]
    tops = [rotated(own_top, "grp", turn) for turn in range(1, groups)]
    (potential,) = call(
        functools.partial(last_term_kernel, sides),
        [node_sums],
        [transfer] + history[-2:] + list(terms),
        flops=8 * dimension * count * count,
        exps=count * count,
        name="last_term",
    )
    (here,) = call(
        functools.partial(far_kernel, len(tops)),
        [block_sums],
        [own_top, potential, product, leaf_interp, near] + tops,
        flops=4 * sides * rows * count,
        name="far_field",
    )
    (out,) = call(total_kernel, [block_sums], [here, back, side], flops=2 * sides * rows, name="total")
    return out


def solution(mesh):
    in_specs = (
        P(None, ("leaf", "grp")),
        P(None, ("leaf", "grp")),
        P(("leaf", "grp")),
        P(("leaf", "grp"), None),
        P(("leaf", "grp"), None, None),
        P(None, ("leaf", "grp")),
        P(("leaf", "grp"), None, None, None),
    )
    out_specs = P(None, ("leaf", "grp"))
    return jax.shard_map(local, mesh=mesh, in_specs=in_specs, out_specs=out_specs, check_vma=False)
```

profile of v0, /device:TPU:0, one launch (start us, length us, event | category | flops | bytes accessed | tf_op | source)
XLA Modules:
  0.0 40.2 jit_solution(6344004700917363959)
XLA Ops:
  0.0 3.0 %collective-permute-start.2 = (bf16[256,1024]{1,0:T(8,128)(2,1)}, bf16[256,1024]{1,0:T(8,128)(2,1)S(1)}, u32[]{:S(2)}, u32[]{:S(2)}) collective-permute-start(bf16[256,1024]{1,0:T(8,128)(2,1)} %wide.3), channel_id=1, source_target_pairs={{0,4},{2,6},{4,8},{6,10},{8,12},{10,14},{12,16},{14,18},{16,20},{1... | collective-permute-start | bytes 1572872 | tf_op jit(solution)/shard_map/ppermute | solution.py:301
  3.0 0.0 copy-start.1
  3.0 3.0 %start.1 = (bf16[64,1024]{1,0:T(8,128)(2,1)}, bf16[256,128]{1,0:T(8,128)(2,1)}, bf16[16,128]{1,0:T(8,128)(2,1)}, bf16[400,128]{1,0:T(8,128)(2,1)}, f32[64,128]{1,0:T(8,128)}) custom-call(s32[1,1024]{1,0:T(1,128)} %bitcast.15, s32[5,1,128]{2,1,0:T(1,128)} %bitcast.10, s32[1,5]{1,0:T(1,128)} %refs_2_.1, bf16[64,1024]{1,0:T(8,128)(2,1)} %refs_3_.1, ...), custom_call_target="tpu_custom_call" | custom-call | tf_op jit(solution)/shard_map/start/pallas_call | solution.py:280
  6.0 1.6 %collective-permute-start = (bf16[400,128]{1,0:T(8,128)(2,1)}, bf16[400,128]{1,0:T(8,128)(2,1)S(1)}, u32[]{:S(2)}, u32[]{:S(2)}) collective-permute-start(bf16[400,128]{1,0:T(8,128)(2,1)} %get-tuple-element.52), channel_id=1, source_target_pairs={{0,2},{2,0},{4,6},{6,4},{8,10},{10,8},{12,14},{14,12},{16,18},{18,... | collective-permute-start | bytes 307208 | tf_op jit(solution)/shard_map/ppermute | solution.py:296
  7.6 0.0 copy-done.1
  7.6 0.0 copy-start.4
  7.6 0.3 turn.2
  7.9 0.6 %copy-done.4 = bf16[64,1024]{1,0:T(8,128)(2,1)S(1)} copy-done((bf16[64,1024]{1,0:T(8,128)(2,1)S(1)}, bf16[64,1024]{1,0:T(8,128)(2,1)}, u32[]{:S(2)}) %copy-start.4) | copy-done | bytes 131096
  8.5 0.0 copy-start
  8.5 0.0 copy-start.3
  8.5 0.0 copy-start.5
  8.5 0.0 copy-start.6
  8.5 1.4 %self_tile.1.near = f32[64,1024]{1,0:T(8,128)S(1)} custom-call(bf16[1024,256]{1,0:T(8,128)(2,1)S(1)} %get-tuple-element.54.tall, f32[1024,128]{1,0:T(8,128)S(1)} %get-tuple-element.55.norms, bf16[256,1024]{1,0:T(8,128)(2,1)S(1)} %copy-done.1, bf16[64,1024]{1,0:T(8,128)(2,1)S(1)} %copy-done.4), custom_call_target="tpu_custom_call" | custom-call | flops 805306368 | bytes 1966080 | tf_op jit(solution)/shard_map/self_tile/pallas_call | solution.py:280
  9.9 1.0 %collective-permute-done.message.refs_1_ = bf16[400,128]{1,0:T(8,128)(2,1)S(1)} collective-permute-done((bf16[400,128]{1,0:T(8,128)(2,1)}, bf16[400,128]{1,0:T(8,128)(2,1)S(1)}, u32[]{:S(2)}, u32[]{:S(2)}) %collective-permute-start) | collective-permute-done | bytes 102432 | tf_op jit(solution)/shard_map/ppermute | solution.py:296
  10.9 1.5 %collective-permute-start.5 = (bf16[256,1024]{1,0:T(8,128)(2,1)S(1)}, bf16[256,1024]{1,0:T(8,128)(2,1)S(1)}, u32[]{:S(2)}, u32[]{:S(2)}) collective-permute-start(bf16[256,1024]{1,0:T(8,128)(2,1)S(1)} %copy-done.1), channel_id=1, source_target_pairs={{0,2},{2,0},{4,6},{6,4},{8,10},{10,8},{12,14},{14,12},{16,18},{18,... | collective-permute-start | bytes 1572872 | tf_op jit(solution)/shard_map/ppermute | solution.py:296
  12.4 0.0 copy-done
  12.4 0.0 copy-done.3
  12.4 0.0 copy-done.5
  12.4 0.0 copy-done.6
  12.4 0.2 join_level.4
  12.7 1.6 %collective-permute-start.1 = (bf16[384,128]{1,0:T(8,128)(2,1)S(1)}, bf16[384,128]{1,0:T(8,128)(2,1)S(1)}, u32[]{:S(2)}, u32[]{:S(2)}) collective-permute-start(bf16[384,128]{1,0:T(8,128)(2,1)S(1)} %get-tuple-element.60), channel_id=1, source_target_pairs={{0,4},{2,6},{4,0},{6,2},{8,12},{10,14},{12,8},{14,10},{16,20},{18,... | collective-permute-start | bytes 294920 | tf_op jit(solution)/shard_map/ppermute | solution.py:296
  14.3 6.0 %collective-permute-done.1.message.refs_3_ = bf16[384,128]{1,0:T(8,128)(2,1)S(1)} collective-permute-done((bf16[384,128]{1,0:T(8,128)(2,1)S(1)}, bf16[384,128]{1,0:T(8,128)(2,1)S(1)}, u32[]{:S(2)}, u32[]{:S(2)}) %collective-permute-start.1) | collective-permute-done | bytes 98336 | tf_op jit(solution)/shard_map/ppermute | solution.py:296
  20.2 0.0 collective-permute-done.2.back_wide
  20.2 0.2 join_level.5
  20.5 0.1 collective-permute-start.4
  20.5 0.3 collective-permute-start.3
  20.8 1.5 %collective-permute-start.6 = (bf16[64,1024]{1,0:T(8,128)(2,1)S(1)}, bf16[64,1024]{1,0:T(8,128)(2,1)S(1)}, u32[]{:S(2)}, u32[]{:S(2)}) collective-permute-start(bf16[64,1024]{1,0:T(8,128)(2,1)S(1)} %copy-done.4), channel_id=1, source_target_pairs={{0,2},{2,0},{4,6},{6,4},{8,10},{10,8},{12,14},{14,12},{16,18},{18,... | collective-permute-start | bytes 393224 | tf_op jit(solution)/shard_map/ppermute | solution.py:296
  22.3 3.0 %collective-permute-done.3.message.refs_5_ = bf16[384,128]{1,0:T(8,128)(2,1)S(1)} collective-permute-done((bf16[384,128]{1,0:T(8,128)(2,1)S(1)}, bf16[384,128]{1,0:T(8,128)(2,1)S(1)}, u32[]{:S(2)}, u32[]{:S(2)}) %collective-permute-start.3) | collective-permute-done | bytes 98336 | tf_op jit(solution)/shard_map/ppermute | solution.py:296
  25.3 0.2 join_level.6
  25.5 0.0 copy-start.7
  25.6 1.2 %collective-permute-start.7 = (bf16[384,128]{1,0:T(8,128)(2,1)S(1)}, bf16[384,128]{1,0:T(8,128)(2,1)S(1)}, u32[]{:S(2)}, u32[]{:S(2)}) collective-permute-start(bf16[384,128]{1,0:T(8,128)(2,1)S(1)} %get-tuple-element.87), channel_id=1, source_target_pairs={{0,16},{2,18},{4,20},{6,22},{8,24},{10,26},{12,28},{14,30},{16,0},... | collective-permute-start | bytes 294920 | tf_op jit(solution)/shard_map/ppermute | solution.py:296
  26.7 0.0 collective-permute-done.5.points
  26.7 0.3 turn.3
  27.1 2.5 %collective-permute-done.4.back_ordered = bf16[64,1024]{1,0:T(8,128)(2,1)S(1)} collective-permute-done((bf16[64,1024]{1,0:T(8,128)(2,1)S(1)}, bf16[64,1024]{1,0:T(8,128)(2,1)S(1)}, u32[]{:S(2)}, u32[]{:S(2)}) %collective-permute-start.4) | collective-permute-done | bytes 131104 | tf_op jit(solution)/shard_map/ppermute | solution.py:301
  29.6 0.0 copy-done.7
  29.6 0.2 back_tile.1
  29.7 0.0 collective-permute-done.6.side_ordered
  29.8 1.9 %pair_tile.1 = (f32[64,1024]{1,0:T(8,128)S(1)}, bf16[64,1024]{1,0:T(8,128)(2,1)S(1)}, bf16[64,1024]{1,0:T(8,128)(2,1)S(1)}) custom-call(bf16[256,1024]{1,0:T(8,128)(2,1)S(1)} %copy-done.1, bf16[64,1024]{1,0:T(8,128)(2,1)S(1)} %copy-done.4, bf16[1024,256]{1,0:T(8,128)(2,1)S(1)} %get-tuple-element.75.side_tall, f32[1024,128]{1,0:T(8,128)S(1)} %get-tuple-element.76.side_norms, ...), custom_call_target="tpu_custom_call" | custom-call | flops 805306368 | bytes 3645440 | tf_op jit(solution)/shard_map/pair_tile/pallas_call | solution.py:280
  31.7 2.1 %collective-permute-start.9 = (bf16[64,1024]{1,0:T(8,128)(2,1)S(1)}, bf16[64,1024]{1,0:T(8,128)(2,1)S(1)}, u32[]{:S(2)}, u32[]{:S(2)}) collective-permute-start(bf16[64,1024]{1,0:T(8,128)(2,1)S(1)} %get-tuple-element.93), channel_id=1, source_target_pairs={{0,28},{2,30},{4,0},{6,2},{8,4},{10,6},{12,8},{14,10},{16,12},{18,... | collective-permute-start | bytes 393224 | tf_op jit(solution)/shard_map/ppermute | solution.py:301
  33.8 0.0 collective-permute-start.10
  33.8 1.0 %early_terms.1 = (f32[64,128]{1,0:T(8,128)S(1)}, f32[64,128]{1,0:T(8,128)S(1)}, f32[64,128]{1,0:T(8,128)S(1)}, f32[128,128]{1,0:T(8,128)S(1)}) custom-call(bf16[4,128,128]{2,1,0:T(8,128)(2,1)S(1)} %bitcast.7, bf16[256,128]{1,0:T(8,128)(2,1)S(1)} %copy-done.3, bf16[400,128]{1,0:T(8,128)(2,1)S(1)} %collective-permute-done.message.refs_1_, ...), custom_call_target="tpu_custom_call" | custom-call | flops 134217728 | bytes 790528 | tf_op jit(solution)/shard_map/early_terms/pallas_call | solution.py:280
  34.8 0.0 collective-permute-done.7.message
  34.8 0.2 join_level.7.own_top
  35.0 0.0 copy-start.2
  35.0 1.8 %collective-permute-start.8 = (bf16[320,128]{1,0:T(8,128)(2,1)S(1)}, bf16[320,128]{1,0:T(8,128)(2,1)S(1)}, u32[]{:S(2)}, u32[]{:S(2)}) collective-permute-start(bf16[320,128]{1,0:T(8,128)(2,1)S(1)} %join_level.7.own_top), channel_id=1, source_target_pairs={{0,1},{1,0},{2,3},{3,2},{4,5},{5,4},{6,7},{7,6},{8,9},{9,8},{10,11... | collective-permute-start | bytes 245768 | tf_op jit(solution)/shard_map/ppermute | solution.py:301
  36.8 0.8 %last_term.1.potential = f32[64,128]{1,0:T(8,128)S(1)} custom-call(bf16[4,128,128]{2,1,0:T(8,128)(2,1)S(1)} %bitcast.9, bf16[256,128]{1,0:T(8,128)(2,1)S(1)} %get-tuple-element.65.coords, bf16[384,128]{1,0:T(8,128)(2,1)S(1)} %collective-permute-done.7.message, f32[64,128]{1,0:T(8,128)S(1)} %get-tuple-element.88.refs_0_, ...), custom_call_target="tpu_custom_call" | custom-call | flops 33554432 | bytes 425984 | tf_op jit(solution)/shard_map/last_term/pallas_call | solution.py:280
  37.7 0.1 collective-permute-done.8.refs_0_
  37.7 0.0 copy-done.2
  37.8 0.9 %far_field.1.here = f32[64,1024]{1,0:T(8,128)S(1)} custom-call(bf16[320,128]{1,0:T(8,128)(2,1)S(1)} %join_level.7.own_top, f32[64,128]{1,0:T(8,128)S(1)} %last_term.1.potential, f32[128,128]{1,0:T(8,128)S(1)} %get-tuple-element.91.product, bf16[128,1024]{1,0:T(8,128)(2,1)S(1)} %copy-done.2, f32[64,1024]{1,0:T(8,128)S(1)} %get-tuple-element.92.near, ...), custom_call_target="tpu_custom_call" | custom-call | flops 33554432 | bytes 1048576 | tf_op jit(solution)/shard_map/far_field/pallas_call | solution.py:280
  38.6 0.0 collective-permute-done.9.back
  38.6 0.9 %collective-permute-done.10.side = bf16[64,1024]{1,0:T(8,128)(2,1)S(1)} collective-permute-done((bf16[64,1024]{1,0:T(8,128)(2,1)S(1)}, bf16[64,1024]{1,0:T(8,128)(2,1)S(1)}, u32[]{:S(2)}, u32[]{:S(2)}) %collective-permute-start.10) | collective-permute-done | bytes 131104 | tf_op jit(solution)/shard_map/ppermute | solution.py:296
  39.5 0.7 %total.1 = f32[64,1024]{1,0:T(8,128)} custom-call(f32[64,1024]{1,0:T(8,128)S(1)} %far_field.1.here, bf16[64,1024]{1,0:T(8,128)(2,1)S(1)} %collective-permute-done.9.back, bf16[64,1024]{1,0:T(8,128)(2,1)S(1)} %collective-permute-done.10.side), custom_call_target="tpu_custom_call" | custom-call | flops 131072 | bytes 786432 | tf_op jit(solution)/shard_map/total/pallas_call | solution.py:280
Async XLA Ops:
  0.0 20.2 %collective-permute-start.2 = (bf16[256,1024]{1,0:T(8,128)(2,1)}, bf16[256,1024]{1,0:T(8,128)(2,1)S(1)}, u32[]{:S(2)}, u32[]{:S(2)}) collective-permute-start(bf16[256,1024]{1,0:T(8,128)(2,1)} %wide.3), channel_id=1, source_target_pairs={{0,4},{2,6},{4,8},{6,10},{8,12},{10,14},{12,16},{14,18},{16,20},{1... | collective-permute-start | bytes 1572872 | tf_op jit(solution)/shard_map/ppermute | solution.py:301
  3.0 4.6 %copy-start.1 = (bf16[256,1024]{1,0:T(8,128)(2,1)S(1)}, bf16[256,1024]{1,0:T(8,128)(2,1)}, u32[]{:S(2)}) copy-start(bf16[256,1024]{1,0:T(8,128)(2,1)} %wide.3) | copy-start | bytes 1572868
  6.0 4.9 %collective-permute-start = (bf16[400,128]{1,0:T(8,128)(2,1)}, bf16[400,128]{1,0:T(8,128)(2,1)S(1)}, u32[]{:S(2)}, u32[]{:S(2)}) collective-permute-start(bf16[400,128]{1,0:T(8,128)(2,1)} %get-tuple-element.52), channel_id=1, source_target_pairs={{0,2},{2,0},{4,6},{6,4},{8,10},{10,8},{12,14},{14,12},{16,18},{18,... | collective-permute-start | bytes 307208 | tf_op jit(solution)/shard_map/ppermute | solution.py:296
  7.6 0.9 %copy-start.4 = (bf16[64,1024]{1,0:T(8,128)(2,1)S(1)}, bf16[64,1024]{1,0:T(8,128)(2,1)}, u32[]{:S(2)}) copy-start(bf16[64,1024]{1,0:T(8,128)(2,1)} %get-tuple-element.68.ordered) | copy-start | bytes 393220
  8.5 4.0 %copy-start = (bf16[1,4,128,128]{3,2,1,0:T(8,128)(2,1)S(1)}, bf16[1,4,128,128]{3,2,1,0:T(8,128)(2,1)}, u32[]{:S(2)}) copy-start(bf16[1,4,128,128]{3,2,1,0:T(8,128)(2,1)} %param.13) | copy-start | bytes 393220
  8.5 4.0 %copy-start.3 = (bf16[256,128]{1,0:T(8,128)(2,1)S(1)}, bf16[256,128]{1,0:T(8,128)(2,1)}, u32[]{:S(2)}) copy-start(bf16[256,128]{1,0:T(8,128)(2,1)} %get-tuple-element.50.coords.refs_0_) | copy-start | bytes 196612
  8.5 4.0 %copy-start.5 = (s32[1,5,128]{2,0,1:T(1,128)S(1)}, s32[1,5,128]{2,0,1:T(1,128)}, u32[]{:S(2)}) copy-start(s32[1,5,128]{2,0,1:T(1,128)} %param.11) | copy-start | bytes 7684
  8.5 4.0 %copy-start.6 = (f32[64,128]{1,0:T(8,128)S(1)}, f32[64,128]{1,0:T(8,128)}, u32[]{:S(2)}) copy-start(f32[64,128]{1,0:T(8,128)} %get-tuple-element.51.passed) | copy-start | bytes 98308
  10.9 15.8 %collective-permute-start.5 = (bf16[256,1024]{1,0:T(8,128)(2,1)S(1)}, bf16[256,1024]{1,0:T(8,128)(2,1)S(1)}, u32[]{:S(2)}, u32[]{:S(2)}) collective-permute-start(bf16[256,1024]{1,0:T(8,128)(2,1)S(1)} %copy-done.1), channel_id=1, source_target_pairs={{0,2},{2,0},{4,6},{6,4},{8,10},{10,8},{12,14},{14,12},{16,18},{18,... | collective-permute-start | bytes 1572872 | tf_op jit(solution)/shard_map/ppermute | solution.py:296
  12.7 7.6 %collective-permute-start.1 = (bf16[384,128]{1,0:T(8,128)(2,1)S(1)}, bf16[384,128]{1,0:T(8,128)(2,1)S(1)}, u32[]{:S(2)}, u32[]{:S(2)}) collective-permute-start(bf16[384,128]{1,0:T(8,128)(2,1)S(1)} %get-tuple-element.60), channel_id=1, source_target_pairs={{0,4},{2,6},{4,0},{6,2},{8,12},{10,14},{12,8},{14,10},{16,20},{18,... | collective-permute-start | bytes 294920 | tf_op jit(solution)/shard_map/ppermute | solution.py:296
  20.5 9.1 %collective-permute-start.4 = (bf16[64,1024]{1,0:T(8,128)(2,1)S(1)}, bf16[64,1024]{1,0:T(8,128)(2,1)S(1)}, u32[]{:S(2)}, u32[]{:S(2)}) collective-permute-start(bf16[64,1024]{1,0:T(8,128)(2,1)S(1)} %copy-done.4), channel_id=1, source_target_pairs={{0,4},{2,6},{4,8},{6,10},{8,12},{10,14},{12,16},{14,18},{16,20},{1... | collective-permute-start | bytes 393224 | tf_op jit(solution)/shard_map/ppermute | solution.py:301
  20.5 4.8 %collective-permute-start.3 = (bf16[384,128]{1,0:T(8,128)(2,1)S(1)}, bf16[384,128]{1,0:T(8,128)(2,1)S(1)}, u32[]{:S(2)}, u32[]{:S(2)}) collective-permute-start(bf16[384,128]{1,0:T(8,128)(2,1)S(1)} %get-tuple-element.64), channel_id=1, source_target_pairs={{0,8},{2,10},{4,12},{6,14},{8,0},{10,2},{12,4},{14,6},{16,24},{18,... | collective-permute-start | bytes 294920 | tf_op jit(solution)/shard_map/ppermute | solution.py:296
  20.8 8.9 %collective-permute-start.6 = (bf16[64,1024]{1,0:T(8,128)(2,1)S(1)}, bf16[64,1024]{1,0:T(8,128)(2,1)S(1)}, u32[]{:S(2)}, u32[]{:S(2)}) collective-permute-start(bf16[64,1024]{1,0:T(8,128)(2,1)S(1)} %copy-done.4), channel_id=1, source_target_pairs={{0,2},{2,0},{4,6},{6,4},{8,10},{10,8},{12,14},{14,12},{16,18},{18,... | collective-permute-start | bytes 393224 | tf_op jit(solution)/shard_map/ppermute | solution.py:296
  25.5 4.0 %copy-start.7 = (bf16[16,128]{1,0:T(8,128)(2,1)S(1)}, bf16[16,128]{1,0:T(8,128)(2,1)}, u32[]{:S(2)}) copy-start(bf16[16,128]{1,0:T(8,128)(2,1)} %get-tuple-element.69.marks) | copy-start | bytes 12292
  25.6 9.2 %collective-permute-start.7 = (bf16[384,128]{1,0:T(8,128)(2,1)S(1)}, bf16[384,128]{1,0:T(8,128)(2,1)S(1)}, u32[]{:S(2)}, u32[]{:S(2)}) collective-permute-start(bf16[384,128]{1,0:T(8,128)(2,1)S(1)} %get-tuple-element.87), channel_id=1, source_target_pairs={{0,16},{2,18},{4,20},{6,22},{8,24},{10,26},{12,28},{14,30},{16,0},... | collective-permute-start | bytes 294920 | tf_op jit(solution)/shard_map/ppermute | solution.py:296
  31.7 6.9 %collective-permute-start.9 = (bf16[64,1024]{1,0:T(8,128)(2,1)S(1)}, bf16[64,1024]{1,0:T(8,128)(2,1)S(1)}, u32[]{:S(2)}, u32[]{:S(2)}) collective-permute-start(bf16[64,1024]{1,0:T(8,128)(2,1)S(1)} %get-tuple-element.93), channel_id=1, source_target_pairs={{0,28},{2,30},{4,0},{6,2},{8,4},{10,6},{12,8},{14,10},{16,12},{18,... | collective-permute-start | bytes 393224 | tf_op jit(solution)/shard_map/ppermute | solution.py:301
  33.8 5.7 %collective-permute-start.10 = (bf16[64,1024]{1,0:T(8,128)(2,1)S(1)}, bf16[64,1024]{1,0:T(8,128)(2,1)S(1)}, u32[]{:S(2)}, u32[]{:S(2)}) collective-permute-start(bf16[64,1024]{1,0:T(8,128)(2,1)S(1)} %get-tuple-element.94), channel_id=1, source_target_pairs={{0,2},{2,0},{4,6},{6,4},{8,10},{10,8},{12,14},{14,12},{16,18},{18,... | collective-permute-start | bytes 393224 | tf_op jit(solution)/shard_map/ppermute | solution.py:296
  35.0 2.8 %copy-start.2 = (bf16[128,1024]{1,0:T(8,128)(2,1)S(1)}, bf16[128,1024]{1,0:T(8,128)(2,1)}, u32[]{:S(2)}) copy-start(bf16[128,1024]{1,0:T(8,128)(2,1)} %interp.1) | copy-start | bytes 786436
  35.0 2.7 %collective-permute-start.8 = (bf16[320,128]{1,0:T(8,128)(2,1)S(1)}, bf16[320,128]{1,0:T(8,128)(2,1)S(1)}, u32[]{:S(2)}, u32[]{:S(2)}) collective-permute-start(bf16[320,128]{1,0:T(8,128)(2,1)S(1)} %join_level.7.own_top), channel_id=1, source_target_pairs={{0,1},{1,0},{2,3},{3,2},{4,5},{5,4},{6,7},{7,6},{8,9},{9,8},{10,11... | collective-permute-start | bytes 245768 | tf_op jit(solution)/shard_map/ppermute | solution.py:301
where the time goes:
time: 40.9 us; the launch traced here: 40.2 us
  starting transfers between devices  14.5 us (35%)
  waiting for transfers between devices  13.5 us (33%)
  Pallas kernels  11.5 us (28%)
  local copies, waits for them, and re-layouts  0.58 us (1%)
    pallas_call x14, Pallas kernels, call(): pl.pallas_call(kernel, out_shape=outs, in_specs=[rest] * len(args), out_s...  11.5 us
    ppermute x7, waiting for transfers between devices, swapped(): lax.ppermute(value, axis, [(place, place ^ flip) for place in range(count)])  10.9 us
    ppermute x7, starting transfers between devices, swapped(): lax.ppermute(value, axis, [(place, place ^ flip) for place in range(count)])  7.58 us
    ppermute x4, starting transfers between devices, rotated(): lax.ppermute(value, axis, [(place, (place + turn) % count) for place in r...  6.96 us
    ppermute x4, waiting for transfers between devices, rotated(): lax.ppermute(value, axis, [(place, (place + turn) % count) for place in r...  2.58 us
  transfers between devices with their start and end apart: 11, of which 6 were waited for; matrix products, arithmetic and copies ran while one was open for 0% of the time, Pallas kernels for 27%

commit v1 on v0

--- a/solution.py
+++ b/solution.py
@@ -13,6 +13,7 @@
 LOG2E = 1.4426950408889634
 HIGHEST = lax.Precision.HIGHEST
 PAD = 16
+JOIN_FLOPS = 500
 VMEM_LIMIT = 40 * 1024 * 1024
 START_VMEM = 56 * 1024 * 1024
 
@@ -170,23 +171,32 @@
     potential_ref[...] = potential
 
 
-def turn_kernel(points, tall_ref, norms_ref):
+def lane_norms(tall):
+    square = jnp.square(tall.astype(F32))
+    norms = jnp.sum(square, axis=1, keepdims=True) * (2.0 * LOG2E / tall.shape[1])
+    return jnp.broadcast_to(norms, (tall.shape[0], 128))
+
+
+def turn_kernel(points, ordered, tall_ref, norms_ref):
     dimension, rows = points.shape
-    tall_ref[...] = jnp.transpose(points[...])
-    square = jnp.square(tall_ref[...].astype(F32))
-    norms = jnp.sum(square, axis=1, keepdims=True) * (2.0 * LOG2E / dimension)
-    norms_ref[...] = jnp.broadcast_to(norms, (rows, 128))
+    sides = ordered.shape[0]
+    tall_ref[:rows] = jnp.transpose(points[...])
+    norms_ref[...] = lane_norms(tall_ref[:rows])
+    for number in range(rows // dimension):
+        first = rows + number * sides
+        tall_ref[first : first + sides] = ordered[:, number * dimension : (number + 1) * dimension]
 
 
 def bands(tall, norms, wide):
-    rows, dimension = tall.shape
+    dimension, rows = wide.shape
     scale = 2.0 * LOG2E / dimension
-    height = min(256, rows)
     target_norms = row_norms(wide[...]) * scale
-    for row in range(0, rows, height):
-        band = slice(row, row + height)
-        inner = dot(tall[band], wide[...])
-        squares = jnp.tile(norms[band], (1, rows // 128)) + target_norms
+    for row in range(0, rows, dimension):
+        band = slice(row, row + dimension)
+        source = tall[band]
+        inner = dot(source, wide[...])
+        own = lane_norms(source) if norms is None else norms[band]
+        squares = jnp.tile(own, (1, rows // 128)) + target_norms
         yield band, jnp.exp2((2.0 * scale) * inner - squares).astype(BF16)
 
 
@@ -195,59 +205,49 @@
         near_ref[:, band] = dot(ordered[...], tile, NT)
 
 
-def back_kernel(tall, norms, ordered, back_wide, back_ordered, marks, near, near_ref, held_ref):
+def near_kernel(tall, norms, wide, ordered, side_tall, back_wide, back_ordered, marks, message,
+                near, near_ref, back_ref, side_ref, held):
+    dimension, rows = wide.shape
+    sides = ordered.shape[0]
+    odd = lax.rem(lax.axis_index("leaf"), 2)
+    with_back = marked(marks[...], -2)
+    go_odd = jnp.logical_and(odd == 1, marked(message[message.shape[0] - PAD :], -1))
+    go_even = jnp.logical_and(odd == 0, marked(marks[...], 1))
     near_ref[...] = near[...]
-    used = marked(marks[...], -2)
-
-    @pl.when(used)
+
+    @pl.when(with_back)
     def _():
         for band, tile in bands(tall, norms, back_wide):
             near_ref[:, band] += dot(back_ordered[...], tile, NT)
             part = dot(ordered[:, band], tile)
             if band.start:
-                held_ref[...] += part
+                held[...] += part
             else:
-                held_ref[...] = part
-
-    @pl.when(jnp.logical_not(used))
+                held[...] = part
+
+    @pl.when(jnp.logical_not(with_back))
     def _():
-        held_ref[...] = jnp.zeros_like(held_ref)
-
-
-def pair_kernel(wide, ordered, side_tall, side_norms, side_ordered, back_wide, back_ordered,
-                marks, message, near, held, near_ref, back_ref, side_ref, sum_ref):
-    odd = lax.rem(lax.axis_index("leaf"), 2)
-    go_odd = jnp.logical_and(odd == 1, marked(message[message.shape[0] - PAD :], -1))
-    go_even = jnp.logical_and(odd == 0, marked(marks[...], 1))
-
-    def pair(other_wide, other_ordered, base, out_ref):
-        for band, tile in bands(side_tall, side_norms, other_wide):
+        held[...] = jnp.zeros_like(held)
+
+    def pair(other_wide, other_ordered, sum_ref):
+        for band, tile in bands(side_tall, None, other_wide):
             side_ref[:, band] = dot(other_ordered[...], tile, NT).astype(BF16)
-            part = dot(side_ordered[:, band], tile)
-            if band.start == 0:
-                part = part + base[...]
-            if band.stop < wide.shape[1]:
-                sum_ref[...] = part if band.start == 0 else sum_ref[...] + part
-            else:
-                if band.start:
-                    part = part + sum_ref[...]
-                out_ref[...] = part.astype(out_ref.dtype)
+            first = rows + band.start // dimension * sides
+            sum_ref[...] += dot(side_tall[first : first + sides], tile)
 
     @pl.when(go_odd)
     def _():
-        pair(back_wide, back_ordered, held, back_ref)
-        near_ref[...] = near[...]
+        pair(back_wide, back_ordered, held)
 
     @pl.when(go_even)
     def _():
-        pair(wide, ordered, near, near_ref)
-        back_ref[...] = held[...].astype(BF16)
+        pair(wide, ordered, near_ref)
 
     @pl.when(jnp.logical_not(jnp.logical_or(go_odd, go_even)))
     def _():
-        near_ref[...] = near[...]
-        back_ref[...] = held[...].astype(BF16)
         side_ref[...] = jnp.zeros_like(side_ref)
+
+    back_ref[...] = held[...].astype(BF16)
 
 
 def far_kernel(others, own_top, potential, product, interp, near, *refs):
@@ -276,7 +276,7 @@
 def call(kernel, outs, args, scratch=(), anywhere=False, flops=0, exps=0, name=None):
     vmem = pl.BlockSpec(memory_space=pltpu.VMEM)
     rest = pl.BlockSpec(memory_space=pl.ANY) if anywhere else vmem
-    moved = 0 if anywhere else sum(a.size * a.dtype.itemsize for a in list(args) + list(outs))
+    moved = 0 if anywhere or flops == 0 else sum(a.size * a.dtype.itemsize for a in list(args) + list(outs))
     return pl.pallas_call(
         kernel,
         out_shape=outs,
@@ -337,22 +337,16 @@
         anywhere=True,
         name="start",
     )
-    def turned(value):
-        return call(
-            turn_kernel,
-            [shape((rows, dimension), BF16), shape((rows, 128), F32)],
-            [value],
-            flops=dimension * rows,
-            name="turn",
-        )
-
-    tall, norms = turned(lax.optimization_barrier((points, passed))[0])
+    tall, norms = call(
+        turn_kernel,
+        [shape((rows + sides * rows // dimension, dimension), BF16), shape((rows, 128), F32)],
+        [points, ordered],
+        name="turn",
+    )
     (near,) = call(
         self_kernel,
         [block_sums],
         [tall, norms, points, ordered],
-        flops=tile_flops,
-        exps=rows * rows,
         name="self_tile",
     )
 
@@ -360,35 +354,23 @@
     for level in range(levels):
         received = swapped(message, "leaf", 1 << level)
         if level == 0:
-            received, near, early_points = lax.optimization_barrier((received, near, points))
+            received, near = lax.optimization_barrier((received, near))
             first_received = received
-            side_points = swapped(early_points, "leaf", 1)
+            side_tall = swapped(tall, "leaf", 1)
         if level == 1:
             received, back_points = lax.optimization_barrier((received, back_points))
         history += [coords, received]
-        if level == levels - 1:
-            near, held = call(
-                back_kernel,
-                [block_sums, block_sums],
-                [tall, norms, ordered, back_points, back_ordered, marks]
-                + [lax.optimization_barrier((near, passed))[0]],
-                flops=tile_flops,
-                exps=rows * rows,
-                name="back_tile",
-            )
-            passed, held = lax.optimization_barrier((passed, held))
         last = level == levels - 1
         if last:
-            side_tall, side_norms = turned(side_points)
             near, back, side = call(
-                pair_kernel,
+                near_kernel,
                 [block_sums, block_values, block_values],
-                [points, ordered, side_tall, side_norms, side_ordered, back_points, back_ordered]
-                + [marks, first_received, lax.optimization_barrier((near, passed))[0], held],
+                [tall, norms, points, ordered, side_tall, back_points, back_ordered]
+                + [marks, first_received, lax.optimization_barrier((near, passed))[0]],
                 scratch=[pltpu.VMEM((sides, rows), F32)],
-                flops=tile_flops,
-                exps=rows * rows,
-                name="pair_tile",
+                flops=2 * tile_flops,
+                exps=2 * rows * rows,
+                name="near_tiles",
             )
             passed, near = lax.optimization_barrier((passed, near))
             back = rotated(back, "leaf", -2)
@@ -410,7 +392,7 @@
             functools.partial(round_kernel, level, last),
             outs,
             [skeletons, transfer, coords, passed, received],
-            flops=8 * dimension * count * count,
+            flops=JOIN_FLOPS * dimension * count * count,
             name="join_level",
         )
         if not last:
@@ -418,7 +400,6 @@
         if level == min(1, levels - 1):
             sent = lax.optimization_barrier((ordered, results[-1]))[0]
             back_ordered = rotated(sent, "leaf", 2)
-            side_ordered = swapped(sent, "leaf", 1)
     own_top = results[0]
     tops = [rotated(own_top, "grp", turn) for turn in range(1, groups)]
     (potential,) = call(

time: 40.9 us -> 38 us (0.929); the launches traced: 40.2 us -> 38.2 us
  starting transfers between devices: 14.5 us -> 7.72 us
  waiting for transfers between devices: 13.5 us -> 17.3 us
  local copies, waits for them, and re-layouts: 0.58 us -> 1.92 us
    ppermute x4, starting transfers between devices: 6.96 us -> 3.1 us  [rotated(): lax.ppermute(value, axis, [(place, (place + turn) % count) for place in r...]
    ppermute x7 -> x6, starting transfers between devices: 7.58 us -> 4.62 us  [swapped(): lax.ppermute(value, axis, [(place, place ^ flip) for place in range(count)])]
    ppermute x4, waiting for transfers between devices: 2.58 us -> 5.51 us  [rotated(): lax.ppermute(value, axis, [(place, (place + turn) % count) for place in r...]
    unnamed x16 -> x18, local copies, waits for them, and re-layouts: 0.58 us -> 1.92 us
    ppermute x7 -> x6, waiting for transfers between devices: 10.9 us -> 11.8 us  [swapped(): lax.ppermute(value, axis, [(place, place ^ flip) for place in range(count)])]
    pallas_call x14 -> x12, Pallas kernels: 11.5 us -> 11.1 us  [call(): pl.pallas_call(kernel, out_shape=outs, in_specs=[rest] * len(args), out_s...]
  transfers between devices with their start and end apart: 11 -> 10, of which waited for: 6 -> 8; matrix products, arithmetic and copies ran while one was open for 0% -> 0% of each run, Pallas kernels for 27% -> 27%
where the time goes in v1:
time: 38 us; the launch traced here: 38.2 us
  waiting for transfers between devices  17.3 us (46%)
  Pallas kernels  11.1 us (29%)
  starting transfers between devices  7.72 us (20%)
  local copies, waits for them, and re-layouts  1.92 us (5%)
    ppermute x6, waiting for transfers between devices, swapped(): lax.ppermute(value, axis, [(place, place ^ flip) for place in range(count)])  11.8 us
    pallas_call x12, Pallas kernels, call(): pl.pallas_call(kernel, out_shape=outs, in_specs=[rest] * len(args), out_s...  11.1 us
    ppermute x4, waiting for transfers between devices, rotated(): lax.ppermute(value, axis, [(place, (place + turn) % count) for place in r...  5.51 us
    ppermute x6, starting transfers between devices, swapped(): lax.ppermute(value, axis, [(place, place ^ flip) for place in range(count)])  4.62 us
    ppermute x4, starting transfers between devices, rotated(): lax.ppermute(value, axis, [(place, (place + turn) % count) for place in r...  3.1 us
    unnamed x18, local copies, waits for them, and re-layouts  1.92 us
  transfers between devices with their start and end apart: 10, of which 8 were waited for; matrix products, arithmetic and copies ran while one was open for 0% of the time, Pallas kernels for 27%

profile of v1, /device:TPU:0, one launch (start us, length us, event | category | flops | bytes accessed | tf_op | source)
XLA Modules:
  0.0 38.2 jit_solution(14185033280768740322)
XLA Ops:
  0.0 3.0 %collective-permute-start.2 = (bf16[256,1024]{1,0:T(8,128)(2,1)}, bf16[256,1024]{1,0:T(8,128)(2,1)S(1)}, u32[]{:S(2)}, u32[]{:S(2)}) collective-permute-start(bf16[256,1024]{1,0:T(8,128)(2,1)} %wide.3), channel_id=1, source_target_pairs={{0,4},{2,6},{4,8},{6,10},{8,12},{10,14},{12,16},{14,18},{16,20},{1... | collective-permute-start | bytes 1572872 | tf_op jit(solution)/shard_map/ppermute | solution.py:301
  3.0 0.0 copy-start
  3.0 3.0 %start.1 = (bf16[64,1024]{1,0:T(8,128)(2,1)}, bf16[256,128]{1,0:T(8,128)(2,1)}, bf16[16,128]{1,0:T(8,128)(2,1)}, bf16[400,128]{1,0:T(8,128)(2,1)}, f32[64,128]{1,0:T(8,128)}) custom-call(s32[1,1024]{1,0:T(1,128)} %bitcast.15, s32[5,1,128]{2,1,0:T(1,128)} %bitcast.10, s32[1,5]{1,0:T(1,128)} %refs_2_.1, bf16[64,1024]{1,0:T(8,128)(2,1)} %refs_3_.1, ...), custom_call_target="tpu_custom_call" | custom-call | tf_op jit(solution)/shard_map/start/pallas_call | solution.py:280
  6.0 1.6 %collective-permute-start = (bf16[400,128]{1,0:T(8,128)(2,1)}, bf16[400,128]{1,0:T(8,128)(2,1)S(1)}, u32[]{:S(2)}, u32[]{:S(2)}) collective-permute-start(bf16[400,128]{1,0:T(8,128)(2,1)} %get-tuple-element.43), channel_id=1, source_target_pairs={{0,2},{2,0},{4,6},{6,4},{8,10},{10,8},{12,14},{14,12},{16,18},{18,... | collective-permute-start | bytes 307208 | tf_op jit(solution)/shard_map/ppermute | solution.py:296
  7.6 0.0 copy-done
  7.6 0.0 copy-start.3
  7.6 0.9 %copy-done.3 = bf16[64,1024]{1,0:T(8,128)(2,1)S(1)} copy-done((bf16[64,1024]{1,0:T(8,128)(2,1)S(1)}, bf16[64,1024]{1,0:T(8,128)(2,1)}, u32[]{:S(2)}) %copy-start.3) | copy-done | bytes 131096
  8.5 0.3 turn.1
  8.8 0.6 %collective-permute-start.4 = (bf16[1280,256]{1,0:T(8,128)(2,1)S(1)}, bf16[1280,256]{1,0:T(8,128)(2,1)S(1)}, u32[]{:S(2)}, u32[]{:S(2)}) collective-permute-start(bf16[1280,256]{1,0:T(8,128)(2,1)S(1)} %get-tuple-element.45.tall), channel_id=1, source_target_pairs={{0,2},{2,0},{4,6},{6,4},{8,10},{10,8},{12,14},{14,12},{16,18},{18,... | collective-permute-start | bytes 1966088 | tf_op jit(solution)/shard_map/ppermute | solution.py:296
  9.4 0.0 copy-start.1
  9.4 0.0 copy-start.5
  9.4 0.0 copy-start.7
  9.4 1.4 %self_tile.1.near = f32[64,1024]{1,0:T(8,128)S(1)} custom-call(bf16[1280,256]{1,0:T(8,128)(2,1)S(1)} %get-tuple-element.45.tall, f32[1024,128]{1,0:T(8,128)S(1)} %get-tuple-element.46.norms, bf16[256,1024]{1,0:T(8,128)(2,1)S(1)} %copy-done, bf16[64,1024]{1,0:T(8,128)(2,1)S(1)} %copy-done.3), custom_call_target="tpu_custom_call" | custom-call | tf_op jit(solution)/shard_map/self_tile/pallas_call | solution.py:280
  10.9 0.0 copy-start.6
  10.9 0.3 collective-permute-done.message.refs_1_
  11.2 0.0 copy-done.1
  11.2 0.0 copy-done.5
  11.2 0.0 copy-done.7
  11.2 0.4 %copy-done.6 = s32[1,5,128]{2,0,1:T(1,128)S(1)} copy-done((s32[1,5,128]{2,0,1:T(1,128)S(1)}, s32[1,5,128]{2,0,1:T(1,128)}, u32[]{:S(2)}) %copy-start.6) | copy-done | bytes 2584
  11.6 0.2 join_level.4
  11.8 1.6 %collective-permute-start.1 = (bf16[384,128]{1,0:T(8,128)(2,1)S(1)}, bf16[384,128]{1,0:T(8,128)(2,1)S(1)}, u32[]{:S(2)}, u32[]{:S(2)}) collective-permute-start(bf16[384,128]{1,0:T(8,128)(2,1)S(1)} %get-tuple-element.50), channel_id=1, source_target_pairs={{0,4},{2,6},{4,0},{6,2},{8,12},{10,14},{12,8},{14,10},{16,20},{18,... | collective-permute-start | bytes 294920 | tf_op jit(solution)/shard_map/ppermute | solution.py:296
  13.4 6.9 %collective-permute-done.1.message.refs_3_ = bf16[384,128]{1,0:T(8,128)(2,1)S(1)} collective-permute-done((bf16[384,128]{1,0:T(8,128)(2,1)S(1)}, bf16[384,128]{1,0:T(8,128)(2,1)S(1)}, u32[]{:S(2)}, u32[]{:S(2)}) %collective-permute-start.1) | collective-permute-done | bytes 98336 | tf_op jit(solution)/shard_map/ppermute | solution.py:296
  20.2 0.0 collective-permute-done.2.back_wide
  20.2 0.0 copy-start.4
  20.2 0.2 join_level.5
  20.5 0.1 collective-permute-start.3
  20.6 0.6 %copy-done.4 = bf16[64,1024]{1,0:T(8,128)(2,1)S(1)} copy-done((bf16[64,1024]{1,0:T(8,128)(2,1)S(1)}, bf16[64,1024]{1,0:T(8,128)(2,1)}, u32[]{:S(2)}) %copy-start.4) | copy-done | bytes 131096
  21.2 0.0 collective-permute-start.5
  21.2 4.1 %collective-permute-done.3.message.refs_5_ = bf16[384,128]{1,0:T(8,128)(2,1)S(1)} collective-permute-done((bf16[384,128]{1,0:T(8,128)(2,1)S(1)}, bf16[384,128]{1,0:T(8,128)(2,1)S(1)}, u32[]{:S(2)}, u32[]{:S(2)}) %collective-permute-start.3) | collective-permute-done | bytes 98336 | tf_op jit(solution)/shard_map/ppermute | solution.py:296
  25.3 0.2 join_level.6
  25.5 0.0 copy-start.8
  25.5 0.7 %collective-permute-start.6 = (bf16[384,128]{1,0:T(8,128)(2,1)S(1)}, bf16[384,128]{1,0:T(8,128)(2,1)S(1)}, u32[]{:S(2)}, u32[]{:S(2)}) collective-permute-start(bf16[384,128]{1,0:T(8,128)(2,1)S(1)} %get-tuple-element.69), channel_id=1, source_target_pairs={{0,16},{2,18},{4,20},{6,22},{8,24},{10,26},{12,28},{14,30},{16,0},... | collective-permute-start | bytes 294920 | tf_op jit(solution)/shard_map/ppermute | solution.py:296
  26.2 1.0 %early_terms.1 = (f32[64,128]{1,0:T(8,128)S(1)}, f32[64,128]{1,0:T(8,128)S(1)}, f32[64,128]{1,0:T(8,128)S(1)}, f32[128,128]{1,0:T(8,128)S(1)}) custom-call(bf16[4,128,128]{2,1,0:T(8,128)(2,1)S(1)} %bitcast.7, bf16[256,128]{1,0:T(8,128)(2,1)S(1)} %copy-done.5, bf16[400,128]{1,0:T(8,128)(2,1)S(1)} %collective-permute-done.message.refs_1_, ...), custom_call_target="tpu_custom_call" | custom-call | flops 134217728 | bytes 790528 | tf_op jit(solution)/shard_map/early_terms/pallas_call | solution.py:280
  27.2 3.1 %collective-permute-done.5.back_ordered = bf16[64,1024]{1,0:T(8,128)(2,1)S(1)} collective-permute-done((bf16[64,1024]{1,0:T(8,128)(2,1)S(1)}, bf16[64,1024]{1,0:T(8,128)(2,1)S(1)}, u32[]{:S(2)}, u32[]{:S(2)}) %collective-permute-start.5) | collective-permute-done | bytes 131104 | tf_op jit(solution)/shard_map/ppermute | solution.py:301
  30.3 0.0 collective-permute-done.4.side_tall
  30.3 0.0 copy-done.8
  30.3 2.0 %near_tiles.1 = (f32[64,1024]{1,0:T(8,128)S(1)}, bf16[64,1024]{1,0:T(8,128)(2,1)S(1)}, bf16[64,1024]{1,0:T(8,128)(2,1)S(1)}) custom-call(bf16[1280,256]{1,0:T(8,128)(2,1)S(1)} %get-tuple-element.45.tall, f32[1024,128]{1,0:T(8,128)S(1)} %get-tuple-element.46.norms, bf16[256,1024]{1,0:T(8,128)(2,1)S(1)} %copy-done, bf16[64,1024]{1,0:T(8,128)(2,1)S(1)} %copy-done.4, ...), custom_call_target="tpu_custom_call" | custom-call | flops 1610612736 | bytes 4038656 | tf_op jit(solution)/shard_map/near_tiles/pallas_call | solution.py:280
  32.4 0.1 collective-permute-start.8
  32.4 0.1 collective-permute-start.9
  32.5 0.5 %collective-permute-done.6.message = bf16[384,128]{1,0:T(8,128)(2,1)S(1)} collective-permute-done((bf16[384,128]{1,0:T(8,128)(2,1)S(1)}, bf16[384,128]{1,0:T(8,128)(2,1)S(1)}, u32[]{:S(2)}, u32[]{:S(2)}) %collective-permute-start.6) | collective-permute-done | bytes 98336 | tf_op jit(solution)/shard_map/ppermute | solution.py:296
  33.0 0.2 join_level.7.own_top
  33.1 0.0 copy-start.2
  33.2 0.1 collective-permute-start.7
  33.2 0.8 %last_term.1.potential = f32[64,128]{1,0:T(8,128)S(1)} custom-call(bf16[4,128,128]{2,1,0:T(8,128)(2,1)S(1)} %bitcast.9, bf16[256,128]{1,0:T(8,128)(2,1)S(1)} %get-tuple-element.55.coords, bf16[384,128]{1,0:T(8,128)(2,1)S(1)} %collective-permute-done.6.message, f32[64,128]{1,0:T(8,128)S(1)} %get-tuple-element.70.refs_0_, ...), custom_call_target="tpu_custom_call" | custom-call | flops 33554432 | bytes 425984 | tf_op jit(solution)/shard_map/last_term/pallas_call | solution.py:280
  34.1 0.4 %collective-permute-done.7.refs_0_ = bf16[320,128]{1,0:T(8,128)(2,1)S(1)} collective-permute-done((bf16[320,128]{1,0:T(8,128)(2,1)S(1)}, bf16[320,128]{1,0:T(8,128)(2,1)S(1)}, u32[]{:S(2)}, u32[]{:S(2)}) %collective-permute-start.7) | collective-permute-done | bytes 81952 | tf_op jit(solution)/shard_map/ppermute | solution.py:301
  34.5 0.0 copy-done.2
  34.5 0.9 %far_field.1.here = f32[64,1024]{1,0:T(8,128)S(1)} custom-call(bf16[320,128]{1,0:T(8,128)(2,1)S(1)} %join_level.7.own_top, f32[64,128]{1,0:T(8,128)S(1)} %last_term.1.potential, f32[128,128]{1,0:T(8,128)S(1)} %get-tuple-element.73.product, bf16[128,1024]{1,0:T(8,128)(2,1)S(1)} %copy-done.2, f32[64,1024]{1,0:T(8,128)S(1)} %get-tuple-element.74.near, ...), custom_call_target="tpu_custom_call" | custom-call | flops 33554432 | bytes 1048576 | tf_op jit(solution)/shard_map/far_field/pallas_call | solution.py:280
  35.4 2.0 %collective-permute-done.8.back = bf16[64,1024]{1,0:T(8,128)(2,1)S(1)} collective-permute-done((bf16[64,1024]{1,0:T(8,128)(2,1)S(1)}, bf16[64,1024]{1,0:T(8,128)(2,1)S(1)}, u32[]{:S(2)}, u32[]{:S(2)}) %collective-permute-start.8) | collective-permute-done | bytes 131104 | tf_op jit(solution)/shard_map/ppermute | solution.py:301
  37.4 0.1 collective-permute-done.9.side
  37.5 0.7 %total.1 = f32[64,1024]{1,0:T(8,128)} custom-call(f32[64,1024]{1,0:T(8,128)S(1)} %far_field.1.here, bf16[64,1024]{1,0:T(8,128)(2,1)S(1)} %collective-permute-done.8.back, bf16[64,1024]{1,0:T(8,128)(2,1)S(1)} %collective-permute-done.9.side), custom_call_target="tpu_custom_call" | custom-call | flops 131072 | bytes 786432 | tf_op jit(solution)/shard_map/total/pallas_call | solution.py:280
Async XLA Ops:
  0.0 20.2 %collective-permute-start.2 = (bf16[256,1024]{1,0:T(8,128)(2,1)}, bf16[256,1024]{1,0:T(8,128)(2,1)S(1)}, u32[]{:S(2)}, u32[]{:S(2)}) collective-permute-start(bf16[256,1024]{1,0:T(8,128)(2,1)} %wide.3), channel_id=1, source_target_pairs={{0,4},{2,6},{4,8},{6,10},{8,12},{10,14},{12,16},{14,18},{16,20},{1... | collective-permute-start | bytes 1572872 | tf_op jit(solution)/shard_map/ppermute | solution.py:301
  3.0 4.6 %copy-start = (bf16[256,1024]{1,0:T(8,128)(2,1)S(1)}, bf16[256,1024]{1,0:T(8,128)(2,1)}, u32[]{:S(2)}) copy-start(bf16[256,1024]{1,0:T(8,128)(2,1)} %wide.3) | copy-start | bytes 1572868
  6.0 5.1 %collective-permute-start = (bf16[400,128]{1,0:T(8,128)(2,1)}, bf16[400,128]{1,0:T(8,128)(2,1)S(1)}, u32[]{:S(2)}, u32[]{:S(2)}) collective-permute-start(bf16[400,128]{1,0:T(8,128)(2,1)} %get-tuple-element.43), channel_id=1, source_target_pairs={{0,2},{2,0},{4,6},{6,4},{8,10},{10,8},{12,14},{14,12},{16,18},{18,... | collective-permute-start | bytes 307208 | tf_op jit(solution)/shard_map/ppermute | solution.py:296
  7.6 0.9 %copy-start.3 = (bf16[64,1024]{1,0:T(8,128)(2,1)S(1)}, bf16[64,1024]{1,0:T(8,128)(2,1)}, u32[]{:S(2)}) copy-start(bf16[64,1024]{1,0:T(8,128)(2,1)} %get-tuple-element.58.ordered) | copy-start | bytes 393220
  8.8 21.5 %collective-permute-start.4 = (bf16[1280,256]{1,0:T(8,128)(2,1)S(1)}, bf16[1280,256]{1,0:T(8,128)(2,1)S(1)}, u32[]{:S(2)}, u32[]{:S(2)}) collective-permute-start(bf16[1280,256]{1,0:T(8,128)(2,1)S(1)} %get-tuple-element.45.tall), channel_id=1, source_target_pairs={{0,2},{2,0},{4,6},{6,4},{8,10},{10,8},{12,14},{14,12},{16,18},{18,... | collective-permute-start | bytes 1966088 | tf_op jit(solution)/shard_map/ppermute | solution.py:296
  9.4 1.7 %copy-start.1 = (bf16[1,4,128,128]{3,2,1,0:T(8,128)(2,1)S(1)}, bf16[1,4,128,128]{3,2,1,0:T(8,128)(2,1)}, u32[]{:S(2)}) copy-start(bf16[1,4,128,128]{3,2,1,0:T(8,128)(2,1)} %param.13) | copy-start | bytes 393220
  9.4 1.7 %copy-start.5 = (bf16[256,128]{1,0:T(8,128)(2,1)S(1)}, bf16[256,128]{1,0:T(8,128)(2,1)}, u32[]{:S(2)}) copy-start(bf16[256,128]{1,0:T(8,128)(2,1)} %get-tuple-element.41.coords.refs_0_) | copy-start | bytes 196612
  9.4 1.7 %copy-start.7 = (f32[64,128]{1,0:T(8,128)S(1)}, f32[64,128]{1,0:T(8,128)}, u32[]{:S(2)}) copy-start(f32[64,128]{1,0:T(8,128)} %get-tuple-element.42.passed) | copy-start | bytes 98308
  10.9 0.7 %copy-start.6 = (s32[1,5,128]{2,0,1:T(1,128)S(1)}, s32[1,5,128]{2,0,1:T(1,128)}, u32[]{:S(2)}) copy-start(s32[1,5,128]{2,0,1:T(1,128)} %param.11) | copy-start | bytes 7684
  11.8 8.5 %collective-permute-start.1 = (bf16[384,128]{1,0:T(8,128)(2,1)S(1)}, bf16[384,128]{1,0:T(8,128)(2,1)S(1)}, u32[]{:S(2)}, u32[]{:S(2)}) collective-permute-start(bf16[384,128]{1,0:T(8,128)(2,1)S(1)} %get-tuple-element.50), channel_id=1, source_target_pairs={{0,4},{2,6},{4,0},{6,2},{8,12},{10,14},{12,8},{14,10},{16,20},{18,... | collective-permute-start | bytes 294920 | tf_op jit(solution)/shard_map/ppermute | solution.py:296
  20.2 0.9 %copy-start.4 = (bf16[64,1024]{1,0:T(8,128)(2,1)S(1)}, bf16[64,1024]{1,0:T(8,128)(2,1)}, u32[]{:S(2)}) copy-start(bf16[64,1024]{1,0:T(8,128)(2,1)} %get-tuple-element.58.ordered) | copy-start | bytes 393220
  20.5 4.8 %collective-permute-start.3 = (bf16[384,128]{1,0:T(8,128)(2,1)S(1)}, bf16[384,128]{1,0:T(8,128)(2,1)S(1)}, u32[]{:S(2)}, u32[]{:S(2)}) collective-permute-start(bf16[384,128]{1,0:T(8,128)(2,1)S(1)} %get-tuple-element.54), channel_id=1, source_target_pairs={{0,8},{2,10},{4,12},{6,14},{8,0},{10,2},{12,4},{14,6},{16,24},{18,... | collective-permute-start | bytes 294920 | tf_op jit(solution)/shard_map/ppermute | solution.py:296
  21.2 9.2 %collective-permute-start.5 = (bf16[64,1024]{1,0:T(8,128)(2,1)S(1)}, bf16[64,1024]{1,0:T(8,128)(2,1)S(1)}, u32[]{:S(2)}, u32[]{:S(2)}) collective-permute-start(bf16[64,1024]{1,0:T(8,128)(2,1)S(1)} %copy-done.4), channel_id=1, source_target_pairs={{0,4},{2,6},{4,8},{6,10},{8,12},{10,14},{12,16},{14,18},{16,20},{1... | collective-permute-start | bytes 393224 | tf_op jit(solution)/shard_map/ppermute | solution.py:301
  25.5 4.8 %copy-start.8 = (bf16[16,128]{1,0:T(8,128)(2,1)S(1)}, bf16[16,128]{1,0:T(8,128)(2,1)}, u32[]{:S(2)}) copy-start(bf16[16,128]{1,0:T(8,128)(2,1)} %get-tuple-element.59.marks) | copy-start | bytes 12292
  25.5 7.5 %collective-permute-start.6 = (bf16[384,128]{1,0:T(8,128)(2,1)S(1)}, bf16[384,128]{1,0:T(8,128)(2,1)S(1)}, u32[]{:S(2)}, u32[]{:S(2)}) collective-permute-start(bf16[384,128]{1,0:T(8,128)(2,1)S(1)} %get-tuple-element.69), channel_id=1, source_target_pairs={{0,16},{2,18},{4,20},{6,22},{8,24},{10,26},{12,28},{14,30},{16,0},... | collective-permute-start | bytes 294920 | tf_op jit(solution)/shard_map/ppermute | solution.py:296
  32.4 5.0 %collective-permute-start.8 = (bf16[64,1024]{1,0:T(8,128)(2,1)S(1)}, bf16[64,1024]{1,0:T(8,128)(2,1)S(1)}, u32[]{:S(2)}, u32[]{:S(2)}) collective-permute-start(bf16[64,1024]{1,0:T(8,128)(2,1)S(1)} %get-tuple-element.75), channel_id=1, source_target_pairs={{0,28},{2,30},{4,0},{6,2},{8,4},{10,6},{12,8},{14,10},{16,12},{18,... | collective-permute-start | bytes 393224 | tf_op jit(solution)/shard_map/ppermute | solution.py:301
  32.4 5.0 %collective-permute-start.9 = (bf16[64,1024]{1,0:T(8,128)(2,1)S(1)}, bf16[64,1024]{1,0:T(8,128)(2,1)S(1)}, u32[]{:S(2)}, u32[]{:S(2)}) collective-permute-start(bf16[64,1024]{1,0:T(8,128)(2,1)S(1)} %get-tuple-element.76), channel_id=1, source_target_pairs={{0,2},{2,0},{4,6},{6,4},{8,10},{10,8},{12,14},{14,12},{16,18},{18,... | collective-permute-start | bytes 393224 | tf_op jit(solution)/shard_map/ppermute | solution.py:296
  33.1 1.4 %copy-start.2 = (bf16[128,1024]{1,0:T(8,128)(2,1)S(1)}, bf16[128,1024]{1,0:T(8,128)(2,1)}, u32[]{:S(2)}) copy-start(bf16[128,1024]{1,0:T(8,128)(2,1)} %interp.1) | copy-start | bytes 786436
  33.2 1.3 %collective-permute-start.7 = (bf16[320,128]{1,0:T(8,128)(2,1)S(1)}, bf16[320,128]{1,0:T(8,128)(2,1)S(1)}, u32[]{:S(2)}, u32[]{:S(2)}) collective-permute-start(bf16[320,128]{1,0:T(8,128)(2,1)S(1)} %join_level.7.own_top), channel_id=1, source_target_pairs={{0,1},{1,0},{2,3},{3,2},{4,5},{5,4},{6,7},{7,6},{8,9},{9,8},{10,11... | collective-permute-start | bytes 245768 | tf_op jit(solution)/shard_map/ppermute | solution.py:301
